TPU v7x, 256 devices: a whole 4x4x8 slice. The times are simulated.
256 devices in a mesh: blk: 64 (over x, z, y_lo), lat: 4 (over y_hi, core).
Axes of the slice: x: 4, y: 4 (y_hi: 2, y_lo: 2; y = y_hi * 2 + y_lo), z: 8, core: 2. Of those that a mesh axis runs over, the one named last changes fastest.
Arguments:
- displacement: float32 [3, 5, 5, 5, 64, 8, 128], P(None, None, None, None, 'blk', 'lat'), may hold values from -6 to 6
- velocity: float32 [3, 5, 5, 5, 64, 8, 128], P(None, None, None, None, 'blk', 'lat'), may hold values from -6 to 6
- rigidity: float32 [5, 5, 5, 64, 8, 128], P(None, None, None, 'blk', 'lat'), may hold values from 0.5 to 2
- density: float32 [5, 5, 5, 64, 8, 128], P(None, None, None, 'blk', 'lat'), may hold values from 0.5 to 2
- history: float32 [256, 63, 3, 128], P(('blk', 'lat')), may hold values from -0.12 to 0.12
- kernel: float32 [64, 3, 3, 128], replicated, may hold values from -0.4375 to 0.4375
- owner_order: int32 [256], replicated, may hold values from 0 to 255, each once
- rigid_offset: float32 [3], replicated, may hold values from -1.8 to 1.8
- rigid_velocity: float32 [3], replicated, may hold values from -6 to 6
Outputs:
- new_displacement: float32 [3, 5, 5, 5, 64, 8, 128], P(None, None, None, None, 'blk', 'lat')
- new_velocity: float32 [3, 5, 5, 5, 64, 8, 128], P(None, None, None, None, 'blk', 'lat')
- new_history: float32 [256, 63, 3, 128], P(('blk', 'lat'))
- new_offset: float32 [3], replicated
- new_rigid_velocity: float32 [3], replicated
Inputs may be any that keep to these rules, and one draw needn't show every extreme that they name: owner_order names every column 0 to 255 once; row j of history belongs to column owner_order[j].
All inputs are finite; a program needn't handle non-finite values.
Results may differ from a plain program's by a relative error of at most 0.0003.
Values sent between devices are 32-bit elements; how exact they have to be, the bound alone decides.
A program may use at most 64 MiB of HBM per device.

v0:
```python
import functools
import math
import jax
import jax.numpy as jnp
import numpy as np
from jax import lax
from jax.sharding import Mesh
from jax.sharding import PartitionSpec as P

STEPS = 3
BLK = ("blk_0", "blk_1", "blk_2")
LAT = ("lat_0", "lat_1")
BLK_LAT = ("blk_0", "blk_1", "blk_2", "lat_0", "lat_1")
pole_gap = 0.1
time_step = 0.03
rigid_gain = 20.0
coupling = 1.0
highest = lax.Precision.HIGHEST


def with_halo(block, sides, width, periodic):
    for axis, dim in sides:
        count = lax.axis_size(axis)
        forward = [(i, i + 1) for i in range(count - 1)]
        if periodic:
            forward.append((count - 1, 0))
        backward = [(target, source) for source, target in forward]
        low = lax.ppermute(
            lax.slice_in_dim(block, block.shape[dim] - width, None, axis=dim), axis, forward
        )
        high = lax.ppermute(lax.slice_in_dim(block, 0, width, axis=dim), axis, backward)
        block = jnp.concatenate([low, block, high], axis=dim)
    return block


def cut_along(shard, dim, length):
    lengths = shard.shape
    parts = shard.reshape(*lengths[:dim], length, lengths[dim] // length, *lengths[dim + 1 :])
    return jnp.moveaxis(parts, dim, 0)


def sum_at_owner(shard, axis, dim):
    parts = cut_along(shard, dim, lax.axis_size(axis))
    arrived = lax.all_to_all(parts, axis, split_axis=0, concat_axis=0, tiled=True)
    return arrived.sum(axis=0)


def over_axes(shard, axes):
    return functools.reduce(lax.psum, axes, shard)


def node_tables():
    points = np.array([-1.0, -math.sqrt(3.0 / 7.0), 0.0, math.sqrt(3.0 / 7.0), 1.0])
    weights = np.array([0.1, 49.0 / 90.0, 32.0 / 45.0, 49.0 / 90.0, 0.1])
    products = np.array(
        [
            np.prod([points[row_at] - points[others] for others in range(5) if others != row_at])
            for row_at in range(5)
        ]
    )
    slopes = np.zeros((5, 5))
    for row_at in range(5):
        for col_at in range(5):
            if row_at == col_at:
                slopes[row_at, col_at] = sum(
                    (
                        1.0 / (points[row_at] - points[others])
                        for others in range(5)
                        if others != row_at
                    )
                )
            else:
                slopes[row_at, col_at] = (
                    products[row_at] / products[col_at] / (points[row_at] - points[col_at])
                )
    return (points, weights, slopes)


def node_volume():
    points, weights, slopes = node_tables()
    node_weight = jnp.asarray(weights, dtype=jnp.float32)
    volume = node_weight[:, None, None] * node_weight[None, :, None] * node_weight[None, None, :]
    return volume[:, :, :, None, None, None]


def stiffness(values, rigidity):
    points, weights, slopes = node_tables()
    deriv = jnp.asarray(slopes, dtype=jnp.float32)
    scaled = (node_volume() * rigidity)[None]
    first_dir = jnp.einsum("ia,kabcxyz->kibcxyz", deriv, values, precision=highest) * scaled
    second_dir = jnp.einsum("jb,kabcxyz->kajcxyz", deriv, values, precision=highest) * scaled
    third_dir = jnp.einsum("lc,kabcxyz->kablxyz", deriv, values, precision=highest) * scaled
    result = jnp.einsum("ia,kibcxyz->kabcxyz", deriv, first_dir, precision=highest)
    result = result + jnp.einsum("jb,kajcxyz->kabcxyz", deriv, second_dir, precision=highest)
    return result + jnp.einsum("lc,kablxyz->kabcxyz", deriv, third_dir, precision=highest)


def join_faces(lower, upper, before_first, after_last, axis):
    count = lower.shape[axis]
    earlier = jnp.concatenate(
        (before_first, lax.slice_in_dim(upper, 0, count - 1, axis=axis)), axis=axis
    )
    later = jnp.concatenate((lax.slice_in_dim(lower, 1, count, axis=axis), after_last), axis=axis)
    return (lower + earlier, upper + later)


def assemble(forces):
    lower, upper = (forces[:, 0], forces[:, 4])
    count = lower.shape[3]
    paired = jnp.concatenate((lower, upper), axis=3)
    widened = with_halo(paired, ((BLK, 3),), 1, True)
    lower, upper = join_faces(
        lower,
        upper,
        lax.slice_in_dim(widened, 0, 1, axis=3),
        lax.slice_in_dim(widened, 3, 4, axis=3),
        3,
    )
    forces = forces.at[:, 0].set(lower).at[:, 4].set(upper)
    lower, upper = (forces[:, :, 0], forces[:, :, 4])
    count = lower.shape[4]
    paired = jnp.concatenate(
        (lax.slice_in_dim(lower, 0, 1, axis=4), lax.slice_in_dim(upper, count - 1, count, axis=4)),
        axis=4,
    )
    widened = with_halo(paired, ((LAT, 4),), 1, False)
    lower, upper = join_faces(
        lower,
        upper,
        lax.slice_in_dim(widened, 0, 1, axis=4),
        lax.slice_in_dim(widened, 3, 4, axis=4),
        4,
    )
    forces = forces.at[:, :, 0].set(lower).at[:, :, 4].set(upper)
    lower, upper = (forces[:, :, :, 0], forces[:, :, :, 4])
    empty = jnp.zeros_like(lax.slice_in_dim(lower, 0, 1, axis=5))
    lower, upper = join_faces(lower, upper, empty, empty, 5)
    return forces.at[:, :, :, 0].set(lower).at[:, :, :, 4].set(upper)


def interface_grid(row_first, row_count, col_first, col_count, lat_elems, lon_elems):
    points, weights, slopes = node_tables()
    nodes = jnp.asarray(points, dtype=jnp.float32)
    node_weight = jnp.asarray(weights, dtype=jnp.float32)
    theta_step = (math.pi - 2.0 * pole_gap) / lat_elems
    phi_step = 2.0 * math.pi / lon_elems
    row_elem = (row_first + jnp.arange(5 * row_count, dtype=jnp.int32) // 5).astype(jnp.float32)
    col_elem = (col_first + jnp.arange(5 * col_count, dtype=jnp.int32) // 5).astype(jnp.float32)
    colatitude = pole_gap + (row_elem + 0.5 * (1.0 + jnp.tile(nodes, row_count))) * theta_step
    longitude = (col_elem + 0.5 * (1.0 + jnp.tile(nodes, col_count))) * phi_step
    row_weight = jnp.tile(node_weight, row_count)
    col_weight = jnp.tile(node_weight, col_count)
    area_weight = (
        0.25
        * theta_step
        * phi_step
        * (row_weight * jnp.sin(colatitude))[:, None]
        * col_weight[None, :]
    )
    face_weight = row_weight[:, None] * col_weight[None, :]
    return (colatitude, longitude, area_weight, face_weight)


def rotation(colatitude, longitude):
    sin_theta = jnp.sin(colatitude)[:, None]
    cos_theta = jnp.cos(colatitude)[:, None]
    sin_phi = jnp.sin(longitude)[None, :]
    cos_phi = jnp.cos(longitude)[None, :]
    filled = jnp.ones((colatitude.shape[0], longitude.shape[0]), jnp.float32)
    radial = (sin_theta * cos_phi, sin_theta * sin_phi, cos_theta * filled)
    polar_dir = (cos_theta * cos_phi, cos_theta * sin_phi, -sin_theta * filled)
    azimuth = (-sin_phi * filled, cos_phi * filled, 0.0 * filled)
    return jnp.stack(
        [jnp.stack([radial[axis_at], polar_dir[axis_at], azimuth[axis_at]]) for axis_at in range(3)]
    )


def legendre(colatitude, degrees):
    cosine = jnp.cos(colatitude)[:, None]
    sine = jnp.sin(colatitude)[:, None]
    orders = jnp.arange(degrees, dtype=jnp.float32)[None, :]
    factor = jnp.where(
        orders == 0,
        math.sqrt(0.5),
        -jnp.sqrt((2.0 * orders + 1.0) / jnp.maximum(2.0 * orders, 1.0)) * sine,
    )
    diagonal = jnp.cumprod(factor, axis=1)

    def advance(state_pair, degree):
        previous, before = state_pair
        level = degree.astype(jnp.float32)
        upward = jnp.sqrt(
            jnp.maximum(4.0 * level * level - 1.0, 0.0)
            / jnp.maximum(level * level - orders * orders, 1.0)
        )
        lowered = (level - 1.0) * (level - 1.0)
        downward = jnp.sqrt(
            jnp.maximum(lowered - orders * orders, 0.0) / jnp.maximum(4.0 * lowered - 1.0, 1.0)
        )
        recurred = upward * (cosine * previous - downward * before)
        values = jnp.where(
            orders == level,
            diagonal,
            jnp.where(
                orders + 1.0 == level,
                jnp.sqrt(2.0 * orders + 3.0) * cosine * diagonal,
                jnp.where(orders + 1.0 < level, recurred, 0.0),
            ),
        )
        return ((values, previous), values)

    zeroed = jnp.zeros((colatitude.shape[0], degrees), jnp.float32)
    finals, levels = lax.scan(advance, (zeroed, zeroed), jnp.arange(degrees, dtype=jnp.int32))
    return levels


def doubled(colatitude, degrees):
    levels = legendre(colatitude, degrees)
    return jnp.concatenate((levels, levels), axis=2)


def circle_table(longitude, degrees):
    orders = jnp.arange(degrees, dtype=jnp.float32)[None, :]
    angles = longitude[:, None] * orders
    cosines = jnp.where(
        orders == 0, 1.0 / math.sqrt(2.0 * math.pi), jnp.cos(angles) / math.sqrt(math.pi)
    )
    sines = jnp.where(orders == 0, 0.0, jnp.sin(angles) / math.sqrt(math.pi))
    return jnp.concatenate((cosines, sines), axis=1)


def synthesize(coeffs, circle, levels):
    partial_value = jnp.einsum("ckl,ltc->ktc", coeffs, levels, precision=highest)
    return jnp.einsum("ktc,fc->ktf", partial_value, circle, precision=highest)


def respond(owned_rows, history, kernel):
    stacked = jnp.concatenate((owned_rows[:, None], history), axis=1)
    replies = jnp.einsum("jabl,cjbl->cal", kernel, stacked, precision=highest)
    return (replies, stacked[:, :-1])


def to_grid(values):
    bottom = values[:, :, :, 0, :, :, 0]
    lon_count, lat_count = (bottom.shape[3], bottom.shape[4])
    return bottom.transpose(0, 4, 2, 3, 1).reshape(3, 5 * lat_count, 5 * lon_count)


def from_grid(grid, lon_count, lat_count):
    return grid.reshape(3, lat_count, 5, lon_count, 5).transpose(0, 4, 2, 3, 1)


def on_device(
    displacement,
    velocity,
    rigidity,
    density,
    history,
    kernel,
    owner_order,
    rigid_offset,
    rigid_velocity,
):
    lon_count, lat_count = (displacement.shape[4], displacement.shape[5])
    blk_count, lat_devices = (lax.axis_size(BLK), lax.axis_size(LAT))
    lon_elems, lat_elems = (lon_count * blk_count, lat_count * lat_devices)
    degrees = kernel.shape[3]
    colatitude, longitude, area_weight, face_weight = interface_grid(
        lax.axis_index(LAT) * lat_count,
        lat_count,
        lax.axis_index(BLK) * lon_count,
        lon_count,
        lat_elems,
        lon_elems,
    )
    rotated = rotation(colatitude, longitude)
    levels = doubled(colatitude, degrees)
    circle = circle_table(longitude, degrees)
    inverse = 1.0 / assemble((density * node_volume())[None])
    block_count = 2 * degrees // blk_count
    circle_ordered = jnp.take(circle, owner_order, axis=1)
    block_columns = lax.dynamic_slice_in_dim(
        owner_order, lax.axis_index(BLK) * block_count, block_count, 0
    )
    levels_block = jnp.take(levels, block_columns, axis=2)
    for step_index in range(STEPS):
        relative = to_grid(displacement) - jnp.einsum(
            "jktf,j->ktf", rotated, rigid_offset, precision=highest
        )
        weighted = relative * area_weight
        block_sums = sum_at_owner(
            jnp.einsum("ktf,fc->ckt", weighted, circle_ordered, precision=highest), BLK, 0
        )
        block_partial = jnp.einsum("ckt,ltc->ckl", block_sums, levels_block, precision=highest)
        owned_rows = sum_at_owner(block_partial, LAT, 0)
        replies, history = respond(owned_rows, history, kernel)
        gathered = lax.all_gather(replies, BLK_LAT, axis=0, tiled=True)
        coeffs = jnp.zeros_like(gathered).at[owner_order].set(gathered)
        traction = synthesize(coeffs, circle, levels)
        pull_sum = over_axes(
            jnp.einsum("jktf,ktf->j", rotated * area_weight, traction, precision=highest), BLK_LAT
        )
        rigid_velocity = rigid_velocity + time_step * rigid_gain * pull_sum
        rigid_offset = rigid_offset + time_step * rigid_velocity
        forces = -stiffness(displacement, rigidity)
        forces = forces.at[:, :, :, 0, :, :, 0].add(
            from_grid(-coupling * face_weight * traction, lon_count, lat_count)
        )
        velocity = velocity + time_step * assemble(forces) * inverse
        displacement = displacement + time_step * velocity
    return (displacement, velocity, history, rigid_offset, rigid_velocity)


def solution(mesh):
    split = Mesh(mesh.devices.reshape(4, 8, 2, 2, 2), ("blk_0", "blk_1", "blk_2", "lat_0", "lat_1"))
    in_specs = (
        P(None, None, None, None, BLK, LAT, None),
        P(None, None, None, None, BLK, LAT, None),
        P(None, None, None, BLK, LAT, None),
        P(None, None, None, BLK, LAT, None),
        P(BLK_LAT, None, None, None),
        P(),
        P(),
        P(),
        P(),
    )
    out_specs = (
        P(None, None, None, None, BLK, LAT, None),
        P(None, None, None, None, BLK, LAT, None),
        P(BLK_LAT, None, None, None),
        P(),
        P(),
    )
    return jax.shard_map(
        on_device, mesh=split, in_specs=in_specs, out_specs=out_specs, check_vma=False
    )
```

profile of v0, /device:TPU:1, one launch (start us, length us, event | category | flops | bytes accessed | tf_op | source)
XLA Modules:
  0.0 1690.9 jit_solution(3025484764923406583)
XLA Ops:
  4.7 2.1 collective-permute-start.4
  6.8 7.5 collective-permute-start.5
  24.4 6.4 all-to-all-start
  32.6 281.5 %while.46 = (s32[]{:T(128)}, f32[10,128]{1,0:T(8,128)S(1)}, f32[10,128]{1,0:T(8,128)S(1)}, f32[128,10,128]{2,1,0:T(8,128)}, s32[128]{0:T(128)S(1)}, /*index=5*/f...) while((s32[]{:T(128)}, f32[10,128]{1,0:T(8,128)S(1)}, ...), condition=%wide.region_2.3_spmd.clone.clone, body=%wide.region_1.2_spmd.clone.clone.sunk | while | flops 14736 | bytes 38715 | solution.py:213
  321.2 2.2 gather_fusion.1
  325.0 6.2 collective-permute-start.6
  331.3 1.9 collective-permute-start.7
  333.3 4.5 collective-permute-done.7
  339.1 3.2 all-to-all-start.1
  343.2 2.2 all-to-all-done.1
  345.5 346.9 %all_gather.9 = f32[256,3,128]{2,1,0:T(4,128)S(1)} all-gather(f32[1,3,128]{2,1,0:T(4,128)S(1)} %bitcast.584), channel_id=1, replica_groups=mesh['blk_0'=4,'blk_1'=8,'blk_2'=2,'lat_0'=2,'lat_1'=2] {'blk_0','blk_1'..., dimensions={0}, use_global_device_ids=true | all-gather | bytes 394752 | tf_op jit(solution)/shard_map/all_gather | solution.py:297
  692.5 7.0 scatter_fusion
  699.5 3.4 convolution_bitcast_fusion.8
  704.7 6.0 psum.105
  710.9 10.7 psum.106
  721.7 3.8 psum.107
  725.5 2.7 collective-permute-start.1
  728.2 5.3 psum.108
  733.5 10.0 psum.109
  744.4 4.1 scatter.101
  748.6 4.1 scatter.104
  752.7 7.1 collective-permute-start.2
  761.2 1.9 collective-permute-start.3
  763.1 5.7 collective-permute-done.3
  771.8 5.2 all-to-all-start.2
  778.6 10.0 all-to-all-done.2
  789.6 5.0 all-to-all-start.3
  796.2 3.0 all-to-all-done.3
  799.3 341.8 %all_gather.10 = f32[256,3,128]{2,1,0:T(4,128)S(1)} all-gather(f32[1,3,128]{2,1,0:T(4,128)S(1)} %bitcast.585), channel_id=1, replica_groups=mesh['blk_0'=4,'blk_1'=8,'blk_2'=2,'lat_0'=2,'lat_1'=2] {'blk_0','blk_1'..., dimensions={0}, use_global_device_ids=true | all-gather | bytes 394752 | tf_op jit(solution)/shard_map/all_gather | solution.py:297
  1141.2 7.0 scatter_fusion.1
  1148.2 3.4 convolution_bitcast_fusion.7
  1153.6 6.1 psum.110
  1161.6 10.7 psum.111
  1172.2 2.7 fusion.61
  1174.9 3.9 psum.112
  1180.3 5.6 psum.113
  1185.9 2.2 fusion.35
  1188.1 9.8 psum.114
  1199.3 2.7 collective-permute-start.9
  1203.5 6.0 collective-permute-done.8
  1209.7 4.0 scatter.124
  1213.7 4.0 scatter.125
  1217.7 5.7 collective-permute-start.10
  1223.4 1.9 collective-permute-start.11
  1225.5 5.0 collective-permute-done.11
  1234.4 4.8 all-to-all-start.4
  1239.9 11.1 all-to-all-done.4
  1252.0 3.2 all-to-all-start.5
  1256.8 1.9 all-to-all-done.5
  1258.9 343.5 %all_gather.11 = f32[256,3,128]{2,1,0:T(4,128)S(1)} all-gather(f32[1,3,128]{2,1,0:T(4,128)S(1)} %bitcast.586), channel_id=1, replica_groups=mesh['blk_0'=4,'blk_1'=8,'blk_2'=2,'lat_0'=2,'lat_1'=2] {'blk_0','blk_1'..., dimensions={0}, use_global_device_ids=true | all-gather | bytes 394752 | tf_op jit(solution)/shard_map/all_gather | solution.py:297
  1602.4 7.0 scatter_fusion.2
  1609.5 3.4 convolution_bitcast_fusion.6
  1614.6 6.1 psum.115
  1621.5 10.7 psum.116
  1634.0 3.8 psum.117
  1638.5 5.4 psum.118
  1644.9 9.8 psum.119
  1656.2 2.7 collective-permute-start.13
  1660.4 7.0 collective-permute-done.12
  1667.6 4.0 scatter.162
  1671.5 4.0 scatter.163
  1675.6 4.2 collective-permute-start.14
  1679.8 1.9 collective-permute-start.15
  1681.9 5.0 collective-permute-done.15
  (1483 shorter events, 261.4 us)
Async XLA Ops:
  0.6 30.2 %copy-start.20 = (f32[5,5,1,1,1,1]{1,0,5,4,3,2:T(8,128)S(1)}, f32[5,5,1,1,1,1]{1,0,5,4,3,2:T(8,128)}, u32[]{:S(2)}) copy-start(f32[5,5,1,1,1,1]{1,0,5,4,3,2:T(8,128)} %constant.794) | copy-start | bytes 304
  0.6 30.2 %copy-start = (f32[3,5,5,5,1,2,128]{6,5,4,3,2,1,0:T(2,128)S(1)}, f32[3,5,5,5,1,2,128]{6,5,4,3,2,1,0:T(2,128)}, u32[]{:S(2)}) copy-start(f32[3,5,5,5,1,2,128]{6,5,4,3,2,1,0:T(2,128)} %param.74) | copy-start | bytes 1152004
  4.0 27.5 %copy-start.29 = (f32[1,5,5,5,1,2,128]{6,5,3,2,4,1,0:T(2,128)}, f32[1,5,5,5,1,2,128]{6,5,3,2,4,1,0:T(2,128)S(1)}, u32[]{:S(2)}) copy-start(f32[1,5,5,5,1,2,128]{6,5,3,2,4,1,0:T(2,128)S(1)} %get-tuple-element.628) | copy-start | bytes 384004
  4.7 318.7 %collective-permute-start.4 = (f32[1,5,5,1,2,128]{5,4,2,1,3,0:T(2,128)}, f32[1,5,5,1,2,128]{5,4,2,1,3,0:T(2,128)}, u32[]{:S(2)}, u32[]{:S(2)}) collective-permute-start(f32[1,5,5,1,2,128]{5,4,2,1,3,0:T(2,128)} %get-tuple-element.636), channel_id=1, source_target_pairs={{0,4},{4,8},{8,12},{12,16},{16,20},{20,24},{24,28},{28,32},{32,36}... | collective-permute-start | bytes 76808 | tf_op jit(solution)/shard_map/ppermute | solution.py:28
  6.8 317.3 %collective-permute-start.5 = (f32[1,5,5,1,2,128]{5,4,2,1,3,0:T(2,128)S(1)}, f32[1,5,5,1,2,128]{5,4,2,1,3,0:T(2,128)}, u32[]{:S(2)}, u32[]{:S(2)}) collective-permute-start(f32[1,5,5,1,2,128]{5,4,2,1,3,0:T(2,128)S(1)} %get-tuple-element.635), channel_id=1, source_target_pairs={{4,0},{8,4},{12,8},{16,12},{20,16},{24,20},{28,24},{32,28},{36,32}... | collective-permute-start | bytes 76808 | tf_op jit(solution)/shard_map/ppermute | solution.py:31
  15.0 1126.2 %copy-start.33 = (s32[256]{0:T(256)}, s32[256]{0:T(256)S(1)}, u32[]{:S(2)}) copy-start(s32[256]{0:T(256)S(1)} %compare_select_fusion) | copy-start | bytes 3076
  15.7 754.7 %copy-start.44 = (pred[256]{0:T(512)(128)(4,1)}, pred[256]{0:T(512)(128)(4,1)S(1)}, u32[]{:S(2)}) copy-start(pred[256]{0:T(512)(128)(4,1)S(1)} %compare_and_fusion.1) | copy-start | bytes 772
  23.5 8.7 copy-start.48
  23.5 9.1 copy-start.52
  24.4 313.8 %all-to-all-start = ((f32[64,4,3,10]{3,1,2,0:T(4,128)}), f32[64,4,3,10]{3,1,2,0:T(4,128)S(1)}, u32[]{:S(2)}, u32[]{:S(2)}) async-start(f32[64,4,3,10]{3,1,2,0:T(4,128)} %copy.581), calls=%async_computation | async-start | bytes 786432 | tf_op jit(solution)/shard_map/all_to_all | solution.py:44
  32.2 756.5 %copy-start.39 = (pred[4]{0:T(512)(128)(4,1)}, pred[4]{0:T(512)(128)(4,1)S(1)}, u32[]{:S(2)}) copy-start(pred[4]{0:T(512)(128)(4,1)S(1)} %get-tuple-element.596) | copy-start | bytes 16
  317.6 861.3 %copy-start.1 = (f32[5,5,5,2,128]{4,0,3,2,1:T(8,128)}, f32[5,5,5,2,128]{4,0,3,2,1:T(8,128)S(1)}, u32[]{:S(2)}) copy-start(f32[5,5,5,2,128]{4,0,3,2,1:T(8,128)S(1)} %copy.561) | copy-start | bytes 384004
  319.3 1.8 copy-start.30
  320.1 3.2 copy-start.27
  321.1 24.2 %copy-start.23 = (f32[1,63,3,128]{3,1,2,0:T(8,128)}, f32[1,63,3,128]{3,1,2,0:T(8,128)S(1)}, u32[]{:S(2)}) copy-start(f32[1,63,3,128]{3,1,2,0:T(8,128)S(1)} %copy.585) | copy-start | bytes 290308
  321.1 24.3 %copy-start.14 = (f32[64,3,3,128]{3,0,2,1:T(8,128)S(1)}, f32[64,3,3,128]{3,0,2,1:T(8,128)}, u32[]{:S(2)}) copy-start(f32[64,3,3,128]{3,0,2,1:T(8,128)} %param.79) | copy-start | bytes 884740
  325.0 8.2 collective-permute-start.6
  331.3 6.5 collective-permute-start.7
  339.1 6.2 all-to-all-start.1
  702.8 57.0 %copy-start.24 = (f32[1,63,3,128]{3,1,2,0:T(8,128)S(1)}, f32[1,63,3,128]{3,1,2,0:T(8,128)}, u32[]{:S(2)}) copy-start(f32[1,63,3,128]{3,1,2,0:T(8,128)} %copy-done.23) | copy-start | bytes 290308
  725.5 23.0 %collective-permute-start.1 = (f32[3,5,5,1,2,128]{5,4,2,1,0,3:T(2,128)S(1)}, f32[3,5,5,1,2,128]{5,4,2,1,0,3:T(2,128)S(1)}, u32[]{:S(2)}, u32[]{:S(2)}) collective-permute-start(f32[3,5,5,1,2,128]{5,4,2,1,0,3:T(2,128)S(1)} %bitcast.558), channel_id=1, source_target_pairs={{4,0},{8,4},{12,8},{16,12},{20,16},{24,20},{28,24},{32,28},{36,32}... | collective-permute-start | bytes 230408 | tf_op jit(solution)/shard_map/ppermute | solution.py:31
  733.5 10.9 collective-permute-start
  743.5 19.6 %copy-start.50 = (f32[3]{0:T(128)}, f32[3]{0:T(128)S(1)}, u32[]{:S(2)}) copy-start(f32[3]{0:T(128)S(1)} %psum.109) | copy-start | bytes 40
  744.2 19.0 %copy-start.41 = (f32[3]{0:T(128)}, f32[3]{0:T(128)S(1)}, u32[]{:S(2)}) copy-start(f32[3]{0:T(128)S(1)} %multiply_add_fusion.8) | copy-start | bytes 40
  752.7 8.4 collective-permute-start.2
  759.9 39.3 %copy-start.25 = (f32[1,63,3,128]{3,1,2,0:T(8,128)}, f32[1,63,3,128]{3,1,2,0:T(8,128)S(1)}, u32[]{:S(2)}) copy-start(f32[1,63,3,128]{3,1,2,0:T(8,128)S(1)} %fusion.99) | copy-start | bytes 290308
  759.9 9.2 copy-start.8
  759.9 9.2 copy-start.11
  761.2 7.7 collective-permute-start.3
  771.8 27.5 %copy-start.15 = (f32[64,3,3,128]{3,0,2,1:T(8,128)S(1)}, f32[64,3,3,128]{3,0,2,1:T(8,128)}, u32[]{:S(2)}) copy-start(f32[64,3,3,128]{3,0,2,1:T(8,128)} %param.79) | copy-start | bytes 884740
  771.8 16.8 all-to-all-start.2
  789.6 9.6 all-to-all-start.3
  799.2 349.0 %copy-start.37 = (f32[1,1,3,128]{3,1,2,0:T(1,128)}, f32[1,1,3,128]{3,1,2,0:T(1,128)S(1)}, u32[]{:S(2)}) copy-start(f32[1,1,3,128]{3,1,2,0:T(1,128)S(1)} %broadcast_in_dim.183) | copy-start | bytes 4612
  1148.2 3.7 copy-start.31
  1148.2 3.9 copy-start.17
  1148.2 3.9 copy-start.19
  1153.6 32.3 %copy-start.35 = (f32[5,5,1,1,1,1]{1,0,2,4,5,3:T(8,128)S(1)}, f32[5,5,1,1,1,1]{1,0,2,4,5,3:T(8,128)}, u32[]{:S(2)}) copy-start(f32[5,5,1,1,1,1]{1,0,2,4,5,3:T(8,128)} %constant.795) | copy-start | bytes 304
  1174.9 23.0 %copy-start.49 = (f32[3]{0:T(128)S(1)}, f32[3]{0:T(128)}, u32[]{:S(2)}) copy-start(f32[3]{0:T(128)} %param.82) | copy-start | bytes 40
  1174.9 23.0 %copy-start.51 = (f32[3]{0:T(128)S(1)}, f32[3]{0:T(128)}, u32[]{:S(2)}) copy-start(f32[3]{0:T(128)} %copy-done.50) | copy-start | bytes 40
  1174.9 23.0 %copy-start.42 = (f32[3]{0:T(128)S(1)}, f32[3]{0:T(128)}, u32[]{:S(2)}) copy-start(f32[3]{0:T(128)} %copy-done.41) | copy-start | bytes 40
  1180.3 21.8 %copy-start.26 = (f32[1,63,3,128]{3,1,2,0:T(8,128)S(1)}, f32[1,63,3,128]{3,1,2,0:T(8,128)}, u32[]{:S(2)}) copy-start(f32[1,63,3,128]{3,1,2,0:T(8,128)} %copy-done.25) | copy-start | bytes 290308
  1180.3 21.8 %copy-start.38 = (f32[1,1,3,128]{3,1,2,0:T(1,128)S(1)}, f32[1,1,3,128]{3,1,2,0:T(1,128)}, u32[]{:S(2)}) copy-start(f32[1,1,3,128]{3,1,2,0:T(1,128)} %copy-done.37) | copy-start | bytes 4612
  1199.3 4.1 collective-permute-start.9
  1202.0 7.5 collective-permute-start.8
  1202.1 56.6 %copy-start.21 = (f32[1,63,3,128]{3,1,2,0:T(8,128)}, f32[1,63,3,128]{3,1,2,0:T(8,128)S(1)}, u32[]{:S(2)}) copy-start(f32[1,63,3,128]{3,1,2,0:T(8,128)S(1)} %fusion.97) | copy-start | bytes 290308
  1217.7 7.7 collective-permute-start.10
  1223.4 7.0 collective-permute-start.11
  1230.8 2.1 copy-start.45
  1232.6 18.6 %copy-start.40 = (pred[4]{0:T(512)(128)(4,1)S(1)}, pred[4]{0:T(512)(128)(4,1)}, u32[]{:S(2)}) copy-start(pred[4]{0:T(512)(128)(4,1)} %copy-done.39) | copy-start | bytes 16
  1234.4 24.5 %copy-start.16 = (f32[64,3,3,128]{3,0,2,1:T(8,128)S(1)}, f32[64,3,3,128]{3,0,2,1:T(8,128)}, u32[]{:S(2)}) copy-start(f32[64,3,3,128]{3,0,2,1:T(8,128)} %param.79) | copy-start | bytes 884740
  1234.4 16.7 all-to-all-start.4
  1239.1 363.3 %copy-start.34 = (s32[256]{0:T(256)S(1)}, s32[256]{0:T(256)}, u32[]{:S(2)}) copy-start(s32[256]{0:T(256)} %copy-done.33) | copy-start | bytes 3076
  1252.0 6.7 all-to-all-start.5
  1609.4 3.7 copy-start.32
  1609.4 3.9 copy-start.2
  1609.4 3.9 copy-start.18
  1614.6 29.3 %copy-start.36 = (f32[5,5,1,1,1,1]{1,0,2,4,5,3:T(8,128)S(1)}, f32[5,5,1,1,1,1]{1,0,2,4,5,3:T(8,128)}, u32[]{:S(2)}) copy-start(f32[5,5,1,1,1,1]{1,0,2,4,5,3:T(8,128)} %constant.795) | copy-start | bytes 304
  1634.0 20.7 %copy-start.43 = (f32[3]{0:T(128)S(1)}, f32[3]{0:T(128)}, u32[]{:S(2)}) copy-start(f32[3]{0:T(128)} %copy-done.41) | copy-start | bytes 40
  1634.0 20.7 %copy-start.47 = (f32[3]{0:T(128)S(1)}, f32[3]{0:T(128)}, u32[]{:S(2)}) copy-start(f32[3]{0:T(128)} %copy-done.46) | copy-start | bytes 40
  1638.5 20.3 %copy-start.22 = (f32[1,63,3,128]{3,1,2,0:T(8,128)S(1)}, f32[1,63,3,128]{3,1,2,0:T(8,128)}, u32[]{:S(2)}) copy-start(f32[1,63,3,128]{3,1,2,0:T(8,128)} %copy-done.21) | copy-start | bytes 290308
  1656.2 4.1 collective-permute-start.13
  1659.6 7.8 collective-permute-start.12
  1675.6 6.2 collective-permute-start.14
  1679.8 7.0 collective-permute-start.15
  (11 other events, 12.3 us)
where the time goes:
time: 1700 us; the launch traced here: 1690 us
  blocking collectives  1140 us (67%)
  local copies, waits for them, and re-layouts  163 us (10%)
  other arithmetic  119 us (7%)
  loops' own time  86.9 us (5%)
  starting transfers between devices  76.8 us (5%)
  waiting for transfers between devices  64.3 us (4%)
  matrix products  38.2 us (2%)
    all_gather x3, blocking collectives, on_device(): gathered = lax.all_gather(replies, BLK_LAT, axis=0, tiled=True)  1030 us
    psum x15, blocking collectives, over_axes(): return functools.reduce(lax.psum, axes, shard)  108 us
    another operation x1, loops' own time, legendre(): lax.scan(advance, (zeroed, zeroed), jnp.arange(degrees, dtype=jnp.int32))  86.9 us
    dynamic_update_slice x128, other arithmetic, legendre(): lax.scan(advance, (zeroed, zeroed), jnp.arange(degrees, dtype=jnp.int32))  86.7 us
    dynamic_slice x128, local copies, waits for them, and re-layouts, legendre(): lax.scan(advance, (zeroed, zeroed), jnp.arange(degrees, dtype=jnp.int32))  82.7 us
  transfers between devices with their start and end apart: 22, of which 14 were waited for; matrix products, arithmetic and copies ran while one was open for 14% of the time, Pallas kernels for 0%

commit v1 on v0

--- a/solution.py
+++ b/solution.py
@@ -294,7 +294,9 @@
         block_partial = jnp.einsum("ckt,ltc->ckl", block_sums, levels_block, precision=highest)
         owned_rows = sum_at_owner(block_partial, LAT, 0)
         replies, history = respond(owned_rows, history, kernel)
-        gathered = lax.all_gather(replies, BLK_LAT, axis=0, tiled=True)
+        gathered = jnp.concatenate(
+            lax.all_to_all(jnp.stack([replies] * lax.axis_size(BLK_LAT)), BLK_LAT, 0, 0), axis=0
+        )
         coeffs = jnp.zeros_like(gathered).at[owner_order].set(gathered)
         traction = synthesize(coeffs, circle, levels)
         pull_sum = over_axes(

time: 1700 us -> 756 us (0.44)
  blocking collectives: 1140 us -> 131 us
  waiting for transfers between devices: 64.3 us -> 100 us
  starting transfers between devices: 76.8 us -> 95.4 us
    all_gather x3 -> x0, blocking collectives: 1030 us -> none  [on_device(): gathered = lax.all_gather(replies, BLK_LAT, axis=0, tiled=True)]
    all_to_all x0 -> x3, waiting for transfers between devices: none -> 46.7 us  [on_device(): lax.all_to_all(jnp.stack([replies] * lax.axis_size(BLK_LAT)), BLK_LAT, 0, 0)]
    all_to_all x0 -> x3, starting transfers between devices: none -> 24.3 us  [on_device(): lax.all_to_all(jnp.stack([replies] * lax.axis_size(BLK_LAT)), BLK_LAT, 0, 0)]
    scatter x3, local copies, waits for them, and re-layouts: 20.9 us -> 39.6 us  [on_device(): coeffs = jnp.zeros_like(gathered).at[owner_order].set(gathered)]
  transfers between devices with their start and end apart: 22 -> 24, of which waited for: 14 -> 15; matrix products, arithmetic and copies ran while one was open for 14% -> 30% of each run, Pallas kernels for 0% -> 0%
where the time goes in v1:
time: 756 us; the launch traced here: 743 us
  local copies, waits for them, and re-layouts  174 us (23%)
  blocking collectives  131 us (17%)
  other arithmetic  122 us (16%)
  waiting for transfers between devices  100 us (13%)
  starting transfers between devices  95.4 us (13%)
  loops' own time  75.7 us (10%)
  matrix products  41.9 us (6%)
    psum x15, blocking collectives, over_axes(): return functools.reduce(lax.psum, axes, shard)  115 us
    dynamic_update_slice x128, other arithmetic, legendre(): lax.scan(advance, (zeroed, zeroed), jnp.arange(degrees, dtype=jnp.int32))  86.7 us
    another operation x1, loops' own time, legendre(): lax.scan(advance, (zeroed, zeroed), jnp.arange(degrees, dtype=jnp.int32))  75.7 us
    dynamic_slice x128, local copies, waits for them, and re-layouts, legendre(): lax.scan(advance, (zeroed, zeroed), jnp.arange(degrees, dtype=jnp.int32))  70.3 us
    all_to_all x3, waiting for transfers between devices, on_device(): lax.all_to_all(jnp.stack([replies] * lax.axis_size(BLK_LAT)), BLK_LAT, 0, 0)  46.7 us
    scatter x3, local copies, waits for them, and re-layouts, on_device(): coeffs = jnp.zeros_like(gathered).at[owner_order].set(gathered)  39.6 us
    ppermute x8, starting transfers between devices, with_halo(): lax.ppermute(lax.slice_in_dim(block, block.shape[dim] - width, None, axis...  27.8 us
    all_to_all x3, starting transfers between devices, on_device(): lax.all_to_all(jnp.stack([replies] * lax.axis_size(BLK_LAT)), BLK_LAT, 0, 0)  24.3 us
  transfers between devices with their start and end apart: 24, of which 15 were waited for; matrix products, arithmetic and copies ran while one was open for 30% of the time, Pallas kernels for 0%

profile of v1, /device:TPU:1, one launch (start us, length us, event | category | flops | bytes accessed | tf_op | source)
XLA Modules:
  0.0 742.6 jit_solution(50296566917709043)
XLA Ops:
  4.7 2.1 collective-permute-start.4
  6.8 7.5 %collective-permute-start.5 = (f32[1,5,5,1,2,128]{5,4,2,1,3,0:T(2,128)}, f32[1,5,5,1,2,128]{5,4,2,1,3,0:T(2,128)}, u32[]{:S(2)}, u32[]{:S(2)}) collective-permute-start(f32[1,5,5,1,2,128]{5,4,2,1,3,0:T(2,128)} %get-tuple-element.645), channel_id=1, source_target_pairs={{4,0},{8,4},{12,8},{16,12},{20,16},{24,20},{28,24},{32,28},{36,32}... | collective-permute-start | bytes 76808 | tf_op jit(solution)/shard_map/ppermute | solution.py:31
  25.0 6.4 all-to-all-start
  33.7 258.0 %while.46 = (s32[]{:T(128)}, f32[10,128]{1,0:T(8,128)S(1)}, f32[10,128]{1,0:T(8,128)S(1)}, f32[128,10,128]{2,1,0:T(8,128)}, s32[128]{0:T(128)S(1)}, /*index=5*/f...) while((s32[]{:T(128)}, f32[10,128]{1,0:T(8,128)S(1)}, ...), condition=%wide.region_2.3_spmd.clone.clone, body=%wide.region_1.2_spmd.clone.clone.sunk | while | flops 14736 | bytes 38715 | solution.py:213
  291.7 1.8 copy.826
  298.7 2.2 gather_fusion.1
  302.5 6.2 collective-permute-start.6
  308.8 1.9 collective-permute-start.7
  312.3 4.9 all-to-all-start.1
  317.3 4.6 all-to-all-done.1
  322.9 10.9 %all-to-all-start.2 = ((f32[256,1,3,128]{3,1,2,0:T(1,128)}), f32[256,1,3,128]{3,1,2,0:T(1,128)S(1)}, u32[]{:S(2)}, u32[]{:S(2)}) async-start(f32[256,1,3,128]{3,1,2,0:T(1,128)} %stack.36), calls=%async_computation.2 | async-start | bytes 786432 | tf_op jit(solution)/shard_map/all_to_all | solution.py:298
  335.0 17.4 %all-to-all-done.2 = f32[256,1,3,128]{3,1,2,0:T(1,128)S(1)} async-done(((f32[256,1,3,128]{3,1,2,0:T(1,128)}), f32[256,1,3,128]{3,1,2,0:T(1,128)S(1)}, u32[]{:S(2)}, u32[]{:S(2)}) %all-to-all-start.2) | async-done | bytes 393248 | tf_op jit(solution)/shard_map/all_to_all | solution.py:298
  352.8 7.0 scatter_fusion
  359.8 3.4 convolution_bitcast_fusion.8
  364.3 6.9 psum.105
  371.4 11.3 %psum.106 = f32[3]{0:T(128)S(1)} all-reduce(f32[3]{0:T(128)S(1)} %psum.105), channel_id=1, replica_groups=mesh['blk_0'=4,'blk_1'=8,'blk_2'=2,'lat_0'=2,'lat_1'=2] {'blk_1'}, use_global_device_ids=true, to_apply=%region_7.8 | all-reduce | flops 3 | bytes 24 | tf_op jit(solution)/shard_map/psum | solution.py:49
  382.8 3.8 psum.107
  387.8 5.3 psum.108
  393.4 11.2 %psum.109 = f32[3]{0:T(128)S(1)} all-reduce(f32[3]{0:T(128)S(1)} %psum.108), channel_id=1, replica_groups=mesh['blk_0'=4,'blk_1'=8,'blk_2'=2,'lat_0'=2,'lat_1'=2] {'lat_1'}, use_global_device_ids=true, to_apply=%region_10.11 | all-reduce | flops 3 | bytes 24 | tf_op jit(solution)/shard_map/psum | solution.py:49
  404.7 4.1 scatter.101
  408.9 4.1 scatter.104
  413.0 8.9 %collective-permute-start.2 = (f32[3,5,5,1,1,128]{5,1,2,0,4,3:T(8,128)S(1)}, f32[3,5,5,1,1,128]{5,1,2,0,4,3:T(8,128)S(1)}, u32[]{:S(2)}, u32[]{:S(2)}) collective-permute-start(f32[3,5,5,1,1,128]{5,1,2,0,4,3:T(8,128)S(1)} %get-tuple-element.659), channel_id=1, source_target_pairs={{0,1},{1,2},{2,3},{4,5},{5,6},{6,7},{8,9},{9,10},{10,11},{12,13},{... | collective-permute-start | bytes 115208 | tf_op jit(solution)/shard_map/ppermute | solution.py:28
  423.3 1.9 collective-permute-start.3
  425.2 5.7 collective-permute-done.3
  434.2 15.7 %all_to_all.45 = f32[64,4,3,10]{3,1,2,0:T(4,128)S(1)} all-to-all(f32[64,4,3,10]{3,1,2,0:T(4,128)S(1)} %copy.888), channel_id=1, replica_groups=mesh['blk_0'=4,'blk_1'=8,'blk_2'=2,'lat_0'=2,'lat_1'=2] {'blk_0','blk_1'..., dimensions={0} | all-to-all | bytes 61440 | tf_op jit(solution)/shard_map/all_to_all | solution.py:44
  450.8 5.0 all-to-all-start.4
  455.8 4.6 all-to-all-done.4
  461.5 5.9 all-to-all-start.5
  470.6 15.3 %all-to-all-done.5 = f32[256,1,3,128]{3,1,2,0:T(1,128)S(1)} async-done(((f32[256,1,3,128]{3,1,2,0:T(1,128)}), f32[256,1,3,128]{3,1,2,0:T(1,128)S(1)}, u32[]{:S(2)}, u32[]{:S(2)}) %all-to-all-start.5) | async-done | bytes 393248 | tf_op jit(solution)/shard_map/all_to_all | solution.py:298
  487.0 16.3 %scatter_fusion.1 = f32[256,3,128]{2,1,0:T(4,128)S(1)} fusion(f32[256,3,128]{2,1,0:T(4,128)S(1)} %broadcast.1226.clone.1, s32[256]{0:T(256)S(1)} %copy-done.40, f32[256,3,128]{2,1,0:T(4,128)} %copy.893), kind=kCustom, calls=%fused_computation.3 | custom fusion | bytes 1180672 | tf_op jit(solution)/shard_map/scatter | solution.py:300
  503.4 3.4 convolution_bitcast_fusion.7
  508.5 7.0 psum.110
  515.5 2.7 fusion.57
  518.2 11.3 %psum.111 = f32[3]{0:T(128)S(1)} all-reduce(f32[3]{0:T(128)S(1)} %psum.110), channel_id=1, replica_groups=mesh['blk_0'=4,'blk_1'=8,'blk_2'=2,'lat_0'=2,'lat_1'=2] {'blk_1'}, use_global_device_ids=true, to_apply=%region_15.16 | all-reduce | flops 3 | bytes 24 | tf_op jit(solution)/shard_map/psum | solution.py:49
  531.0 4.1 psum.112
  536.7 5.4 psum.113
  542.1 2.4 fusion.35
  544.5 10.4 %psum.114 = f32[3]{0:T(128)S(1)} all-reduce(f32[3]{0:T(128)S(1)} %psum.113), channel_id=1, replica_groups=mesh['blk_0'=4,'blk_1'=8,'blk_2'=2,'lat_0'=2,'lat_1'=2] {'lat_1'}, use_global_device_ids=true, to_apply=%region_18.19 | all-reduce | flops 3 | bytes 24 | tf_op jit(solution)/shard_map/psum | solution.py:49
  560.0 6.1 collective-permute-done.8
  566.2 4.0 scatter.124
  570.2 4.0 scatter.125
  574.3 4.6 collective-permute-start.10
  578.9 1.9 collective-permute-start.11
  581.0 5.0 collective-permute-done.11
  591.2 4.6 all-to-all-start.6
  596.6 11.2 %all-to-all-done.6 = f32[64,4,3,10]{3,1,2,0:T(4,128)S(1)} async-done(((f32[64,4,3,10]{3,1,2,0:T(4,128)}), f32[64,4,3,10]{3,1,2,0:T(4,128)S(1)}, u32[]{:S(2)}, u32[]{:S(2)}) %all-to-all-start.6) | async-done | bytes 30752 | tf_op jit(solution)/shard_map/all_to_all | solution.py:44
  608.8 3.2 all-to-all-start.7
  612.8 2.7 all-to-all-done.7
  617.5 7.5 %all-to-all-start.8 = ((f32[256,1,3,128]{3,1,2,0:T(1,128)}), f32[256,1,3,128]{3,1,2,0:T(1,128)}, u32[]{:S(2)}, u32[]{:S(2)}) async-start(f32[256,1,3,128]{3,1,2,0:T(1,128)} %stack.38), calls=%async_computation.8 | async-start | bytes 786432 | tf_op jit(solution)/shard_map/all_to_all | solution.py:298
  628.5 14.0 %all-to-all-done.8 = f32[256,1,3,128]{3,1,2,0:T(1,128)} async-done(((f32[256,1,3,128]{3,1,2,0:T(1,128)}), f32[256,1,3,128]{3,1,2,0:T(1,128)}, u32[]{:S(2)}, u32[]{:S(2)}) %all-to-all-start.8) | async-done | bytes 393248 | tf_op jit(solution)/shard_map/all_to_all | solution.py:298
  644.8 16.3 %scatter_fusion.2 = f32[256,3,128]{2,1,0:T(4,128)S(1)} fusion(f32[256,3,128]{2,1,0:T(4,128)S(1)} %broadcast.1226, s32[256]{0:T(256)S(1)} %copy-done.41, f32[256,3,128]{2,1,0:T(4,128)} %copy.928), kind=kCustom, calls=%fused_computation.4 | custom fusion | bytes 1180672 | tf_op jit(solution)/shard_map/scatter | solution.py:300
  661.1 3.4 convolution_bitcast_fusion.6
  665.9 6.9 psum.115
  674.3 11.6 %psum.116 = f32[3]{0:T(128)S(1)} all-reduce(f32[3]{0:T(128)S(1)} %psum.115), channel_id=1, replica_groups=mesh['blk_0'=4,'blk_1'=8,'blk_2'=2,'lat_0'=2,'lat_1'=2] {'blk_1'}, use_global_device_ids=true, to_apply=%region_23.24 | all-reduce | flops 3 | bytes 24 | tf_op jit(solution)/shard_map/psum | solution.py:49
  685.8 2.0 fusion.40
  687.8 3.8 psum.117
  691.7 5.3 psum.118
  697.7 10.6 %psum.119 = f32[3]{0:T(128)S(1)} all-reduce(f32[3]{0:T(128)S(1)} %psum.118), channel_id=1, replica_groups=mesh['blk_0'=4,'blk_1'=8,'blk_2'=2,'lat_0'=2,'lat_1'=2] {'lat_1'}, use_global_device_ids=true, to_apply=%region_26.27 | all-reduce | flops 3 | bytes 24 | tf_op jit(solution)/shard_map/psum | solution.py:49
  713.1 5.8 collective-permute-done.12
  719.0 4.0 scatter.162
  723.0 4.0 scatter.163
  727.0 4.9 collective-permute-start.14
  731.9 1.9 collective-permute-start.15
  734.0 5.0 collective-permute-done.15
  (1514 shorter events, 261.1 us)
Async XLA Ops:
  0.6 30.8 %copy-start.17 = (f32[5,5,1,1,1,1]{1,0,5,4,3,2:T(8,128)S(1)}, f32[5,5,1,1,1,1]{1,0,5,4,3,2:T(8,128)}, u32[]{:S(2)}) copy-start(f32[5,5,1,1,1,1]{1,0,5,4,3,2:T(8,128)} %constant.794) | copy-start | bytes 304
  0.6 30.8 %copy-start = (f32[3,5,5,5,1,2,128]{6,5,4,3,2,1,0:T(2,128)S(1)}, f32[3,5,5,5,1,2,128]{6,5,4,3,2,1,0:T(2,128)}, u32[]{:S(2)}) copy-start(f32[3,5,5,5,1,2,128]{6,5,4,3,2,1,0:T(2,128)} %param.74) | copy-start | bytes 1152004
  4.0 18.8 %copy-start.24 = (f32[1,5,5,5,1,2,128]{6,5,3,2,4,1,0:T(2,128)}, f32[1,5,5,5,1,2,128]{6,5,3,2,4,1,0:T(2,128)S(1)}, u32[]{:S(2)}) copy-start(f32[1,5,5,5,1,2,128]{6,5,3,2,4,1,0:T(2,128)S(1)} %get-tuple-element.638) | copy-start | bytes 384004
  4.7 296.2 %collective-permute-start.4 = (f32[1,5,5,1,2,128]{5,4,2,1,3,0:T(2,128)}, f32[1,5,5,1,2,128]{5,4,2,1,3,0:T(2,128)}, u32[]{:S(2)}, u32[]{:S(2)}) collective-permute-start(f32[1,5,5,1,2,128]{5,4,2,1,3,0:T(2,128)} %get-tuple-element.646), channel_id=1, source_target_pairs={{0,4},{4,8},{8,12},{12,16},{16,20},{20,24},{24,28},{28,32},{32,36}... | collective-permute-start | bytes 76808 | tf_op jit(solution)/shard_map/ppermute | solution.py:28
  6.8 294.9 %collective-permute-start.5 = (f32[1,5,5,1,2,128]{5,4,2,1,3,0:T(2,128)}, f32[1,5,5,1,2,128]{5,4,2,1,3,0:T(2,128)}, u32[]{:S(2)}, u32[]{:S(2)}) collective-permute-start(f32[1,5,5,1,2,128]{5,4,2,1,3,0:T(2,128)} %get-tuple-element.645), channel_id=1, source_target_pairs={{4,0},{8,4},{12,8},{16,12},{20,16},{24,20},{28,24},{32,28},{36,32}... | collective-permute-start | bytes 76808 | tf_op jit(solution)/shard_map/ppermute | solution.py:31
  15.7 16.4 %copy-start.53 = (pred[256]{0:T(512)(128)(4,1)}, pred[256]{0:T(512)(128)(4,1)S(1)}, u32[]{:S(2)}) copy-start(pred[256]{0:T(512)(128)(4,1)S(1)} %compare_and_fusion.1) | copy-start | bytes 772
  19.4 13.4 %copy-start.29 = (f32[10,5]{0,1:T(8,128)}, f32[10,5]{0,1:T(8,128)S(1)}, u32[]{:S(2)}) copy-start(f32[10,5]{0,1:T(8,128)S(1)} %get-tuple-element.671) | copy-start | bytes 604
  20.7 12.0 %copy-start.25 = (f32[5,128]{1,0:T(8,128)}, f32[5,128]{1,0:T(8,128)S(1)}, u32[]{:S(2)}) copy-start(f32[5,128]{1,0:T(8,128)S(1)} %get-tuple-element.669) | copy-start | bytes 7684
  25.0 285.8 %all-to-all-start = ((f32[64,4,3,10]{3,1,2,0:T(4,128)}), f32[64,4,3,10]{3,1,2,0:T(4,128)S(1)}, u32[]{:S(2)}, u32[]{:S(2)}) async-start(f32[64,4,3,10]{3,1,2,0:T(4,128)} %copy.834), calls=%async_computation | async-start | bytes 786432 | tf_op jit(solution)/shard_map/all_to_all | solution.py:44
  298.6 23.3 %copy-start.9 = (f32[64,3,3,128]{3,0,2,1:T(8,128)S(1)}, f32[64,3,3,128]{3,0,2,1:T(8,128)}, u32[]{:S(2)}) copy-start(f32[64,3,3,128]{3,0,2,1:T(8,128)} %param.79) | copy-start | bytes 884740
  298.7 24.3 %copy-start.18 = (f32[1,63,3,128]{3,1,2,0:T(8,128)}, f32[1,63,3,128]{3,1,2,0:T(8,128)S(1)}, u32[]{:S(2)}) copy-start(f32[1,63,3,128]{3,1,2,0:T(8,128)S(1)} %copy.838) | copy-start | bytes 290308
  302.5 8.2 %collective-permute-start.6 = (f32[1,5,5,1,1,128]{5,4,3,2,1,0:T(1,128)S(1)}, f32[1,5,5,1,1,128]{5,4,3,2,1,0:T(1,128)S(1)}, u32[]{:S(2)}, u32[]{:S(2)}) collective-permute-start(f32[1,5,5,1,1,128]{5,4,3,2,1,0:T(1,128)S(1)} %get-tuple-element.665), channel_id=1, source_target_pairs={{0,1},{1,2},{2,3},{4,5},{5,6},{6,7},{8,9},{9,10},{10,11},{12,13},{... | collective-permute-start | bytes 38408 | tf_op jit(solution)/shard_map/ppermute | solution.py:28
  308.8 8.4 %collective-permute-start.7 = (f32[1,5,5,1,1,128]{5,4,3,2,1,0:T(1,128)S(1)}, f32[1,5,5,1,1,128]{5,4,3,2,1,0:T(1,128)S(1)}, u32[]{:S(2)}, u32[]{:S(2)}) collective-permute-start(f32[1,5,5,1,1,128]{5,4,3,2,1,0:T(1,128)S(1)} %get-tuple-element.664), channel_id=1, source_target_pairs={{1,0},{2,1},{3,2},{5,4},{6,5},{7,6},{9,8},{10,9},{11,10},{13,12},{... | collective-permute-start | bytes 38408 | tf_op jit(solution)/shard_map/ppermute | solution.py:31
  312.3 9.5 %all-to-all-start.1 = ((f32[4,1,3,128]{3,1,2,0:T(1,128)}), f32[4,1,3,128]{3,1,2,0:T(1,128)S(1)}, u32[]{:S(2)}, u32[]{:S(2)}) async-start(f32[4,1,3,128]{3,1,2,0:T(1,128)} %copy.837), calls=%async_computation.1 | async-start | bytes 12288 | tf_op jit(solution)/shard_map/all_to_all | solution.py:44
  321.9 30.8 %copy-start.44 = (f32[1,1,3,128]{3,1,2,0:T(1,128)}, f32[1,1,3,128]{3,1,2,0:T(1,128)S(1)}, u32[]{:S(2)}) copy-start(f32[1,1,3,128]{3,1,2,0:T(1,128)S(1)} %broadcast_in_dim.181) | copy-start | bytes 4612
  322.9 29.8 %copy-start.39 = (s32[256]{0:T(256)S(1)}, s32[256]{0:T(256)}, u32[]{:S(2)}) copy-start(s32[256]{0:T(256)} %copy-done.38) | copy-start | bytes 3076
  322.9 29.4 %all-to-all-start.2 = ((f32[256,1,3,128]{3,1,2,0:T(1,128)}), f32[256,1,3,128]{3,1,2,0:T(1,128)S(1)}, u32[]{:S(2)}, u32[]{:S(2)}) async-start(f32[256,1,3,128]{3,1,2,0:T(1,128)} %stack.36), calls=%async_computation.2 | async-start | bytes 786432 | tf_op jit(solution)/shard_map/all_to_all | solution.py:298
  352.7 10.5 %copy-start.26 = (f32[5,128]{1,0:T(8,128)S(1)}, f32[5,128]{1,0:T(8,128)}, u32[]{:S(2)}) copy-start(f32[5,128]{1,0:T(8,128)} %copy-done.25) | copy-start | bytes 7684
  352.8 10.8 %copy-start.35 = (f32[3,3,10,5]{2,1,3,0:T(4,128)S(1)}, f32[3,3,10,5]{2,1,3,0:T(4,128)}, u32[]{:S(2)}) copy-start(f32[3,3,10,5]{2,1,3,0:T(4,128)} %get-tuple-element.661) | copy-start | bytes 5404
  359.8 44.8 %copy-start.57 = (f32[3]{0:T(128)S(1)}, f32[3]{0:T(128)}, u32[]{:S(2)}) copy-start(f32[3]{0:T(128)} %param.81) | copy-start | bytes 40
  359.8 44.8 %copy-start.58 = (f32[3]{0:T(128)S(1)}, f32[3]{0:T(128)}, u32[]{:S(2)}) copy-start(f32[3]{0:T(128)} %param.82) | copy-start | bytes 40
  386.6 22.2 %collective-permute-start.1 = (f32[3,5,5,1,2,128]{5,4,2,1,0,3:T(2,128)S(1)}, f32[3,5,5,1,2,128]{5,4,2,1,0,3:T(2,128)S(1)}, u32[]{:S(2)}, u32[]{:S(2)}) collective-permute-start(f32[3,5,5,1,2,128]{5,4,2,1,0,3:T(2,128)S(1)} %bitcast.576), channel_id=1, source_target_pairs={{4,0},{8,4},{12,8},{16,12},{20,16},{24,20},{28,24},{32,28},{36,32}... | collective-permute-start | bytes 230408 | tf_op jit(solution)/shard_map/ppermute | solution.py:31
  393.0 11.6 %collective-permute-start = (f32[3,5,5,1,2,128]{5,4,2,1,0,3:T(2,128)S(1)}, f32[3,5,5,1,2,128]{5,4,2,1,0,3:T(2,128)S(1)}, u32[]{:S(2)}, u32[]{:S(2)}) collective-permute-start(f32[3,5,5,1,2,128]{5,4,2,1,0,3:T(2,128)S(1)} %bitcast.574), channel_id=1, source_target_pairs={{0,4},{4,8},{8,12},{12,16},{16,20},{20,24},{24,28},{28,32},{32,36}... | collective-permute-start | bytes 230408 | tf_op jit(solution)/shard_map/ppermute | solution.py:28
  404.6 26.3 %copy-start.50 = (f32[3]{0:T(128)}, f32[3]{0:T(128)S(1)}, u32[]{:S(2)}) copy-start(f32[3]{0:T(128)S(1)} %multiply_add_fusion.8) | copy-start | bytes 40
  413.0 10.2 %collective-permute-start.2 = (f32[3,5,5,1,1,128]{5,1,2,0,4,3:T(8,128)S(1)}, f32[3,5,5,1,1,128]{5,1,2,0,4,3:T(8,128)S(1)}, u32[]{:S(2)}, u32[]{:S(2)}) collective-permute-start(f32[3,5,5,1,1,128]{5,1,2,0,4,3:T(8,128)S(1)} %get-tuple-element.659), channel_id=1, source_target_pairs={{0,1},{1,2},{2,3},{4,5},{5,6},{6,7},{8,9},{9,10},{10,11},{12,13},{... | collective-permute-start | bytes 115208 | tf_op jit(solution)/shard_map/ppermute | solution.py:28
  423.3 7.7 %collective-permute-start.3 = (f32[3,5,5,1,1,128]{5,1,2,0,4,3:T(8,128)S(1)}, f32[3,5,5,1,1,128]{5,1,2,0,4,3:T(8,128)S(1)}, u32[]{:S(2)}, u32[]{:S(2)}) collective-permute-start(f32[3,5,5,1,1,128]{5,1,2,0,4,3:T(8,128)S(1)} %get-tuple-element.656), channel_id=1, source_target_pairs={{1,0},{2,1},{3,2},{5,4},{6,5},{7,6},{9,8},{10,9},{11,10},{13,12},{... | collective-permute-start | bytes 115208 | tf_op jit(solution)/shard_map/ppermute | solution.py:31
  431.5 18.5 %copy-start.48 = (pred[4]{0:T(512)(128)(4,1)S(1)}, pred[4]{0:T(512)(128)(4,1)}, u32[]{:S(2)}) copy-start(pred[4]{0:T(512)(128)(4,1)} %get-tuple-element.606) | copy-start | bytes 16
  431.5 24.3 %copy-start.19 = (f32[1,63,3,128]{3,1,2,0:T(8,128)S(1)}, f32[1,63,3,128]{3,1,2,0:T(8,128)}, u32[]{:S(2)}) copy-start(f32[1,63,3,128]{3,1,2,0:T(8,128)} %copy-done.18) | copy-start | bytes 290308
  431.5 24.3 %copy-start.45 = (f32[1,1,3,128]{3,1,2,0:T(1,128)S(1)}, f32[1,1,3,128]{3,1,2,0:T(1,128)}, u32[]{:S(2)}) copy-start(f32[1,1,3,128]{3,1,2,0:T(1,128)} %copy-done.44) | copy-start | bytes 4612
  431.5 28.9 %copy-start.10 = (f32[64,3,3,128]{3,0,2,1:T(8,128)S(1)}, f32[64,3,3,128]{3,0,2,1:T(8,128)}, u32[]{:S(2)}) copy-start(f32[64,3,3,128]{3,0,2,1:T(8,128)} %param.79) | copy-start | bytes 884740
  450.8 9.6 %all-to-all-start.4 = ((f32[4,1,3,128]{3,1,2,0:T(1,128)}), f32[4,1,3,128]{3,1,2,0:T(1,128)S(1)}, u32[]{:S(2)}, u32[]{:S(2)}) async-start(f32[4,1,3,128]{3,1,2,0:T(1,128)} %copy.891), calls=%async_computation.4 | async-start | bytes 12288 | tf_op jit(solution)/shard_map/all_to_all | solution.py:44
  455.8 14.8 %copy-start.20 = (f32[1,63,3,128]{3,1,2,0:T(8,128)}, f32[1,63,3,128]{3,1,2,0:T(8,128)S(1)}, u32[]{:S(2)}) copy-start(f32[1,63,3,128]{3,1,2,0:T(8,128)S(1)} %fusion.99) | copy-start | bytes 290308
  461.5 24.4 %all-to-all-start.5 = ((f32[256,1,3,128]{3,1,2,0:T(1,128)}), f32[256,1,3,128]{3,1,2,0:T(1,128)S(1)}, u32[]{:S(2)}, u32[]{:S(2)}) async-start(f32[256,1,3,128]{3,1,2,0:T(1,128)} %stack.37), calls=%async_computation.5 | async-start | bytes 786432 | tf_op jit(solution)/shard_map/all_to_all | solution.py:298
  467.4 19.7 %copy-start.40 = (s32[256]{0:T(256)S(1)}, s32[256]{0:T(256)}, u32[]{:S(2)}) copy-start(s32[256]{0:T(256)} %copy-done.38) | copy-start | bytes 3076
  486.9 19.8 %copy-start.27 = (f32[5,128]{1,0:T(8,128)S(1)}, f32[5,128]{1,0:T(8,128)}, u32[]{:S(2)}) copy-start(f32[5,128]{1,0:T(8,128)} %copy-done.25) | copy-start | bytes 7684
  486.9 19.8 %copy-start.33 = (f32[10,5]{0,1:T(8,128)S(1)}, f32[10,5]{0,1:T(8,128)}, u32[]{:S(2)}) copy-start(f32[10,5]{0,1:T(8,128)} %get-tuple-element.670) | copy-start | bytes 604
  487.0 20.0 %copy-start.36 = (f32[3,3,10,5]{2,1,3,0:T(4,128)S(1)}, f32[3,3,10,5]{2,1,3,0:T(4,128)}, u32[]{:S(2)}) copy-start(f32[3,3,10,5]{2,1,3,0:T(4,128)} %get-tuple-element.661) | copy-start | bytes 5404
  508.5 33.6 %copy-start.42 = (f32[5,5,1,1,1,1]{1,0,2,4,5,3:T(8,128)S(1)}, f32[5,5,1,1,1,1]{1,0,2,4,5,3:T(8,128)}, u32[]{:S(2)}) copy-start(f32[5,5,1,1,1,1]{1,0,2,4,5,3:T(8,128)} %constant.795) | copy-start | bytes 304
  531.0 23.8 %copy-start.59 = (f32[3]{0:T(128)S(1)}, f32[3]{0:T(128)}, u32[]{:S(2)}) copy-start(f32[3]{0:T(128)} %param.82) | copy-start | bytes 40
  531.0 23.8 %copy-start.61 = (f32[3]{0:T(128)S(1)}, f32[3]{0:T(128)}, u32[]{:S(2)}) copy-start(f32[3]{0:T(128)} %copy-done.60) | copy-start | bytes 40
  536.7 21.1 %copy-start.51 = (f32[3]{0:T(128)S(1)}, f32[3]{0:T(128)}, u32[]{:S(2)}) copy-start(f32[3]{0:T(128)} %copy-done.50) | copy-start | bytes 40
  554.8 19.4 %copy-start.54 = (f32[3]{0:T(128)}, f32[3]{0:T(128)S(1)}, u32[]{:S(2)}) copy-start(f32[3]{0:T(128)S(1)} %multiply_add_fusion.7) | copy-start | bytes 40
  556.2 3.7 collective-permute-start.9
  558.6 7.5 %collective-permute-start.8 = (f32[3,5,5,1,2,128]{5,4,2,1,0,3:T(2,128)S(1)}, f32[3,5,5,1,2,128]{5,4,2,1,0,3:T(2,128)S(1)}, u32[]{:S(2)}, u32[]{:S(2)}) collective-permute-start(f32[3,5,5,1,2,128]{5,4,2,1,0,3:T(2,128)S(1)} %bitcast.582), channel_id=1, source_target_pairs={{0,4},{4,8},{8,12},{12,16},{16,20},{20,24},{24,28},{28,32},{32,36}... | collective-permute-start | bytes 230408 | tf_op jit(solution)/shard_map/ppermute | solution.py:28
  574.3 6.6 collective-permute-start.10
  578.9 7.0 collective-permute-start.11
  587.9 20.1 %copy-start.49 = (pred[4]{0:T(512)(128)(4,1)S(1)}, pred[4]{0:T(512)(128)(4,1)}, u32[]{:S(2)}) copy-start(pred[4]{0:T(512)(128)(4,1)} %get-tuple-element.606) | copy-start | bytes 16
  589.0 27.5 %copy-start.11 = (f32[64,3,3,128]{3,0,2,1:T(8,128)S(1)}, f32[64,3,3,128]{3,0,2,1:T(8,128)}, u32[]{:S(2)}) copy-start(f32[64,3,3,128]{3,0,2,1:T(8,128)} %param.79) | copy-start | bytes 884740
  591.2 16.6 %all-to-all-start.6 = ((f32[64,4,3,10]{3,1,2,0:T(4,128)}), f32[64,4,3,10]{3,1,2,0:T(4,128)S(1)}, u32[]{:S(2)}, u32[]{:S(2)}) async-start(f32[64,4,3,10]{3,1,2,0:T(4,128)} %copy.923), calls=%async_computation.6 | async-start | bytes 786432 | tf_op jit(solution)/shard_map/all_to_all | solution.py:44
  608.8 6.7 all-to-all-start.7
  617.5 25.1 %all-to-all-start.8 = ((f32[256,1,3,128]{3,1,2,0:T(1,128)}), f32[256,1,3,128]{3,1,2,0:T(1,128)}, u32[]{:S(2)}, u32[]{:S(2)}) async-start(f32[256,1,3,128]{3,1,2,0:T(1,128)} %stack.38), calls=%async_computation.8 | async-start | bytes 786432 | tf_op jit(solution)/shard_map/all_to_all | solution.py:298
  626.9 17.8 %copy-start.41 = (s32[256]{0:T(256)S(1)}, s32[256]{0:T(256)}, u32[]{:S(2)}) copy-start(s32[256]{0:T(256)} %copy-done.38) | copy-start | bytes 3076
  644.7 19.8 %copy-start.28 = (f32[5,128]{1,0:T(8,128)S(1)}, f32[5,128]{1,0:T(8,128)}, u32[]{:S(2)}) copy-start(f32[5,128]{1,0:T(8,128)} %copy-done.25) | copy-start | bytes 7684
  644.7 19.8 %copy-start.34 = (f32[10,5]{0,1:T(8,128)S(1)}, f32[10,5]{0,1:T(8,128)}, u32[]{:S(2)}) copy-start(f32[10,5]{0,1:T(8,128)} %get-tuple-element.670) | copy-start | bytes 604
  644.8 20.0 %copy-start.37 = (f32[3,3,10,5]{2,1,3,0:T(4,128)S(1)}, f32[3,3,10,5]{2,1,3,0:T(4,128)}, u32[]{:S(2)}) copy-start(f32[3,3,10,5]{2,1,3,0:T(4,128)} %get-tuple-element.661) | copy-start | bytes 5404
  664.5 21.3 %copy-start.12 = (f32[3,5,5,2,128,5]{4,5,3,2,1,0:T(8,128)S(1)}, f32[3,5,5,2,128,5]{4,5,3,2,1,0:T(8,128)}, u32[]{:S(2)}) copy-start(f32[3,5,5,2,128,5]{4,5,3,2,1,0:T(8,128)} %fusion.49) | copy-start | bytes 1152004
  664.5 21.3 %copy-start.43 = (f32[5,5,1,1,1,1]{1,0,2,4,5,3:T(8,128)S(1)}, f32[5,5,1,1,1,1]{1,0,2,4,5,3:T(8,128)}, u32[]{:S(2)}) copy-start(f32[5,5,1,1,1,1]{1,0,2,4,5,3:T(8,128)} %constant.795) | copy-start | bytes 304
  665.9 25.8 %copy-start.22 = (f32[1,63,3,128]{3,1,2,0:T(8,128)S(1)}, f32[1,63,3,128]{3,1,2,0:T(8,128)}, u32[]{:S(2)}) copy-start(f32[1,63,3,128]{3,1,2,0:T(8,128)} %fusion.97) | copy-start | bytes 290308
  674.3 36.3 %copy-start.52 = (f32[3]{0:T(128)S(1)}, f32[3]{0:T(128)}, u32[]{:S(2)}) copy-start(f32[3]{0:T(128)} %copy-done.50) | copy-start | bytes 40
  674.3 36.3 %copy-start.55 = (f32[3]{0:T(128)S(1)}, f32[3]{0:T(128)}, u32[]{:S(2)}) copy-start(f32[3]{0:T(128)} %copy-done.54) | copy-start | bytes 40
  709.3 3.7 collective-permute-start.13
  711.2 7.7 %collective-permute-start.12 = (f32[3,5,5,1,2,128]{5,4,2,1,0,3:T(2,128)S(1)}, f32[3,5,5,1,2,128]{5,4,2,1,0,3:T(2,128)S(1)}, u32[]{:S(2)}, u32[]{:S(2)}) collective-permute-start(f32[3,5,5,1,2,128]{5,4,2,1,0,3:T(2,128)S(1)} %bitcast.583), channel_id=1, source_target_pairs={{0,4},{4,8},{8,12},{12,16},{16,20},{20,24},{24,28},{28,32},{32,36}... | collective-permute-start | bytes 230408 | tf_op jit(solution)/shard_map/ppermute | solution.py:28
  727.0 6.8 collective-permute-start.14
  731.9 7.0 collective-permute-start.15
  (23 other events, 116.1 us)
